TPU v7x, 512 devices: a whole 4x4x16 slice. The times are simulated.
512 devices in a mesh: ctx: 64 (over z, x), tp: 8 (over y, core).
Axes of the slice: x: 4, y: 4, z: 16, core: 2. Of those that a mesh axis runs over, the one named last changes fastest.
Arguments:
- tokens: bfloat16 [65536, 4096], P(('ctx', 'tp')), may hold values from -26 to 26
- query_weight: bfloat16 [4096, 2048], P('ctx', 'tp'), may hold values from -0.09375 to 0.09375
- kv_weight: bfloat16 [4096, 2048], P('ctx', 'tp'), may hold values from -0.09375 to 0.09375
- reach: int32 [1024], P('ctx'), may hold values from 1 to 2, as said below
- global_ids: int32 [2], replicated, may hold values from 0 to 1023, as said below
- rand_ids: int32 [1024, 3], replicated, may hold values from -1 to 1023, as said below
Outputs:
- attended: bfloat16 [65536, 2048], P('ctx', 'tp')
Inputs may be any that keep to these rules, and one draw needn't show every extreme that they name: Some query block has reach 2. `global_ids`: distinct block numbers; the last entry is block 1023. `rand_ids`: the -1 entries of a query block come after its other entries; the 16 query blocks of a run (blocks 16 * i to 16 * i + 15) list at most 2 entries, repeats counted, that name blocks of any one run; in some run all entries are filled and some run of key blocks is named by exactly 2 of them.
All inputs are finite; a program needn't handle non-finite values.
Results may differ from a plain program's by a relative error of at most 0.012.
The roundings to bfloat16 on the way count: a program that leaves them out, or rounds other values in their place, can miss the bound.
Values may be sent and summed in bfloat16 or wider, within the bound.
No kernel may reach another device: no remote copies, remote signals or barrier semaphores. Data moves between devices by JAX's collectives and lax.ppermute only.
A program may use at most 64 MiB of HBM per device.

v0:
```python
import jax
import jax.numpy as jnp
from jax import lax
from jax.sharding import PartitionSpec as P

HD = 128
GROUP = 2
BS = 64
WMAX = 2
G = 2
masked_score = -1e30


def with_halo(shard, sides, width):
    for axis, dim in sides:
        size, length = (lax.axis_size(axis), shard.shape[dim])
        up = [(i, (i + 1) % size) for i in range(size - 1)]
        down = [(j, i) for i, j in up]
        last = lax.slice_in_dim(shard, length - width, length, axis=dim)
        initial = lax.slice_in_dim(shard, 0, width, axis=dim)
        before = lax.ppermute(last, axis, up)
        after = lax.ppermute(initial, axis, down)
        shard = jnp.concatenate([before, shard, after], axis=dim)
    return shard


def attend_group(query_group, slab_group, valid_group, kv_local):
    group_blocks = query_group.shape[0]
    slot_count = slab_group.shape[1]
    queries = query_group.reshape(group_blocks, BS, kv_local, GROUP, HD)
    slabs = slab_group.reshape(group_blocks, slot_count, BS, kv_local, 2, HD)
    scores = jnp.einsum(
        "bqkgd,bsjkd->bkgqsj", queries, slabs[:, :, :, :, 0, :], preferred_element_type=jnp.float32
    )
    scores = scores.reshape(scores.shape[:4] + (slot_count * BS,)) * HD ** (-0.5)
    key_live = jnp.repeat(valid_group, BS, axis=1)
    scores = jnp.where(key_live[:, None, None, None, :], scores, masked_score)
    row_max = jnp.max(scores, axis=-1, keepdims=True)
    exponent = jnp.exp(scores - row_max)
    weights = (exponent / jnp.sum(exponent, axis=-1, keepdims=True)).astype(jnp.bfloat16)
    weights = weights.reshape(weights.shape[:4] + (slot_count, BS))
    mixed = jnp.einsum(
        "bkgqsj,bsjkd->bqkgd", weights, slabs[:, :, :, :, 1, :], preferred_element_type=jnp.float32
    )
    return mixed.astype(jnp.bfloat16).reshape(group_blocks * BS, kv_local * GROUP * HD)


def fetch_blocks(key_rows, global_ids, rand_ids, ctx_index, ctx_count):
    row_count, lane_width = key_rows.shape
    run_blocks = row_count // BS
    blocks = key_rows.reshape(run_blocks, BS, lane_width)
    padded = with_halo(key_rows, (("ctx", 0),), WMAX * BS)
    padded_blocks = padded.reshape(run_blocks + 2 * WMAX, BS, lane_width)
    window_kv = jnp.stack(
        [padded_blocks[shift_at : shift_at + run_blocks] for shift_at in range(2 * WMAX + 1)],
        axis=1,
    )
    global_owner = global_ids // run_blocks
    global_local = global_ids % run_blocks
    is_held = (global_owner == ctx_index)[:, None, None]
    sum_term = jnp.where(is_held, blocks[global_local].astype(jnp.float32), 0.0)
    global_kv = lax.psum(sum_term, "ctx").astype(jnp.bfloat16)
    slot_count = run_blocks * rand_ids.shape[1]
    capacity = max(2, (slot_count + ctx_count - 1) // ctx_count)
    listed = rand_ids.reshape(ctx_count, slot_count)
    owners = jnp.where(listed >= 0, listed // run_blocks, -1)
    owned_here = owners == ctx_index
    ranks = jnp.cumsum(owned_here.astype(jnp.int32), axis=1) - 1
    picks = owned_here[:, None, :] & (ranks[:, None, :] == jnp.arange(capacity)[None, :, None])
    local_ids = jnp.sum(jnp.where(picks, listed[:, None, :] % run_blocks, 0), axis=2)
    filled = jnp.any(picks, axis=2)
    outgoing = jnp.where(filled[:, :, None, None], blocks[local_ids], jnp.zeros((), jnp.bfloat16))
    incoming = lax.all_to_all(outgoing, "ctx", split_axis=0, concat_axis=0, tiled=True)
    wanted = lax.dynamic_index_in_dim(owners, ctx_index, 0, keepdims=False)
    slot_order = jnp.arange(slot_count)
    earlier = (wanted[None, :] == wanted[:, None]) & (slot_order[None, :] < slot_order[:, None])
    position = jnp.sum(earlier.astype(jnp.int32), axis=1)
    flat_index = jnp.where(wanted >= 0, wanted * capacity + position, 0)
    random_kv = incoming.reshape(ctx_count * capacity, BS, lane_width)[flat_index]
    random_kv = random_kv.reshape(run_blocks, -1, BS, lane_width)
    return (window_kv, global_kv, random_kv)


def per_device(tokens, query_weight, kv_weight, reach, global_ids, rand_ids):
    ctx_count = lax.axis_size("ctx")
    ctx_index = lax.axis_index("ctx")
    full_query_w, full_kv_w = (
        lax.all_gather(query_weight, "ctx", axis=0, tiled=True),
        lax.all_gather(kv_weight, "ctx", axis=0, tiled=True),
    )
    query_width = full_query_w.shape[1]
    token_piece = lax.all_gather(tokens, "tp", axis=0, tiled=True)
    query_part = jnp.dot(token_piece, full_query_w, preferred_element_type=jnp.float32)
    key_part = jnp.dot(token_piece, full_kv_w, preferred_element_type=jnp.float32)
    projected = jnp.concatenate([query_part, key_part], axis=1)
    query_rows = projected[:, :query_width].astype(jnp.bfloat16)
    key_rows = projected[:, query_width:].astype(jnp.bfloat16)
    window_kv, global_kv, random_kv = fetch_blocks(
        key_rows, global_ids, rand_ids, ctx_index, ctx_count
    )
    row_count, lane_width = key_rows.shape
    run_blocks = row_count // BS
    kv_local = lane_width // (2 * HD)
    offsets = jnp.arange(-WMAX, WMAX + 1)
    first_block = ctx_index * run_blocks
    target = first_block + jnp.arange(run_blocks)[:, None] + offsets[None, :]
    window_live = (
        (jnp.abs(offsets)[None, :] <= reach[:, None])
        & (target >= 0)
        & (target < run_blocks * ctx_count)
    )
    own_lists = lax.dynamic_slice_in_dim(rand_ids, first_block, run_blocks, 0)
    slot_valid = jnp.concatenate(
        [window_live, jnp.ones((run_blocks, G), jnp.bool_), own_lists >= 0], axis=1
    )
    global_tiled = jnp.broadcast_to(global_kv[None], (run_blocks,) + global_kv.shape)
    slab_all = jnp.concatenate([window_kv, global_tiled, random_kv], axis=1)
    slot_total = slab_all.shape[1]
    group_size = max((divisor for divisor in range(1, 9) if run_blocks % divisor == 0))
    group_count = run_blocks // group_size
    query_groups = query_rows.reshape(group_count, group_size, BS, query_width)
    slab_groups = slab_all.reshape(group_count, group_size, slot_total, BS, lane_width)
    valid_groups = slot_valid.reshape(group_count, group_size, slot_total)

    def one_group(operands):
        return attend_group(operands[0], operands[1], operands[2], kv_local)

    outputs = lax.map(one_group, (query_groups, slab_groups, valid_groups))
    return outputs.reshape(row_count, query_width)


def solution(mesh):
    in_specs = (P(("ctx", "tp"), None), P("ctx", "tp"), P("ctx", "tp"), P("ctx"), P(), P())
    out_specs = P("ctx", "tp")
    return jax.shard_map(
        per_device, mesh=mesh, in_specs=in_specs, out_specs=out_specs, check_vma=False
    )
```

profile of v0, /device:TPU:8, one launch (start us, length us, event | category | flops | bytes accessed | tf_op | source)
XLA Modules:
  0.0 769.2 jit_solution(11982867577212984012)
XLA Ops:
  6.5 0.7 all-gather.6.cloned.1.call-update
  7.3 0.0 all-gather.4.cloned.1.call-start
  7.3 0.7 all-gather.4.cloned.1.call-update
  8.0 0.9 copy.68
  9.0 0.3 reshape.282
  9.2 0.1 copy.72
  9.3 0.2 reduce_window_sum.11
  9.6 0.1 copy.70
  9.6 0.1 copy.69
  9.8 0.1 copy.71
  9.9 0.1 copy.73
  10.0 0.1 reshape.297
  10.2 0.7 compare_select_fusion.2
  10.9 144.8 %all-gather.6.cloned.1.call-done = bf16[4096,256]{1,0:T(8,128)(2,1)} async-done(((bf16[64,256]{1,0:T(8,128)(2,1)}), bf16[4096,256]{1,0:T(8,128)(2,1)}) %all-gather.6.cloned.1.call-update) | async-done | bytes 2097168 | tf_op jit(solution)/shard_map/all_gather | solution.py:89
  155.7 54.8 %all-gather.4.cloned.1.call-done = bf16[1024,4096]{1,0:T(8,128)(2,1)} async-done(((bf16[128,4096]{1,0:T(8,128)(2,1)}), bf16[1024,4096]{1,0:T(8,128)(2,1)}) %all-gather.4.cloned.1.call-update) | async-done | bytes 8388624 | tf_op jit(solution)/shard_map/all_gather | solution.py:92
  210.4 6.3 convolution_convert_fusion.1
  216.8 2.7 gather_fusion.1
  219.5 4.5 broadcast_select_fusion
  224.0 16.0 %all-to-all-start = ((bf16[64,2,64,256]{3,2,1,0:T(8,128)(2,1)}), bf16[64,2,64,256]{3,2,1,0:T(8,128)(2,1)}, u32[]{:S(2)}, u32[]{:S(2)}) async-start(bf16[64,2,64,256]{3,2,1,0:T(8,128)(2,1)} %broadcast_select_fusion), calls=%async_computation | async-start | bytes 8388608 | tf_op jit(solution)/shard_map/all_to_all | solution.py:73
  240.0 0.0 all-gather.8.cloned.1.call-start
  240.1 0.7 all-gather.8.cloned.1.call-update
  240.8 0.1 pad.1.clone
  240.9 0.8 dynamic-slice_compare_fusion
  241.6 0.1 fusion.35
  241.7 0.1 pad_add_fusion
  241.8 0.1 copy.79
  241.9 0.2 convert_reduce_fusion
  242.1 1.3 collective-permute-start.1
  243.4 4.5 collective-permute-start
  248.0 0.6 gather_fusion
  248.6 0.1 convert_select_fusion
  248.6 184.2 %all-gather.8.cloned.1.call-done = bf16[4096,256]{1,0:T(8,128)(2,1)} async-done(((bf16[64,256]{1,0:T(8,128)(2,1)}), bf16[4096,256]{1,0:T(8,128)(2,1)}) %all-gather.8.cloned.1.call-update) | async-done | bytes 2097168 | tf_op jit(solution)/shard_map/all_gather | solution.py:88
  432.9 6.3 convolution_convert_fusion
  439.2 279.7 %all-reduce.1 = bf16[2,64,256]{2,1,0:T(8,128)(2,1)S(1)} all-reduce(f32[2,64,256]{2,1,0:T(8,128)S(1)} %convert_select_fusion), channel_id=1, replica_groups=mesh['ctx'=64,'tp'=8] {'ctx'}, use_global_device_ids=true, to_apply=%region_0.1 | all-reduce | flops 32768 | bytes 196608 | tf_op jit(solution)/shard_map/psum | solution.py:62
  718.9 0.1 pad_maximum_fusion
  719.1 0.9 constant_dynamic-update-slice_fusion.6
  720.0 0.9 constant_dynamic-update-slice_fusion.5
  720.8 0.9 constant_dynamic-update-slice_fusion.4
  721.7 0.9 constant_dynamic-update-slice_fusion.3
  722.6 0.9 constant_dynamic-update-slice_fusion.2
  723.4 1.1 broadcast_dynamic-update-slice_fusion
  724.5 2.8 gather_fusion.2
  727.4 1.3 constant_dynamic-update-slice_fusion.1
  728.7 34.0 %while.10 = (s32[]{:T(128)}, bf16[2,512,256]{2,1,0:T(8,128)(2,1)}, bf16[2,8,10,64,256]{4,3,2,1,0:T(8,128)(2,1)}, pred[2,8,10]{2,1,0:T(8,128)(4,1)S(1)}, bf16[2,8,64,256]{3,2,1,0:T(8,128)(2,1)S(1)}, /*index=5*/s32[]{:T(128)}) while((s32[]{:T(128)}, bf16[2,512,256]{2,1,0:T(8,128)(2,1)}, bf16[2,8,10,64,256]{4,3,2,1,0:T(8,128)(2,1)}, ...), condition=%wide.region_8.9_spmd, body=%wide.region_5.8_spmd.sunk | while | flops 343537664 | bytes 33575460 | solution.py:128
  728.7 0.1 reshape.319
  728.8 3.6 constant_dynamic-slice_fusion.6
  732.3 3.5 reshape.320
  735.9 3.7 fusion.55
  739.6 1.3 bitcast_reduce_fusion.2
  740.9 1.5 fusion.56
  742.4 1.9 fusion.57
  744.4 0.3 copy.115
  744.6 0.2 broadcast_in_dim.143
  744.9 0.8 copy-done.2
  745.7 0.1 reshape.319
  745.7 3.6 constant_dynamic-slice_fusion.6
  749.3 3.5 reshape.320
  752.9 3.7 fusion.55
  756.6 1.3 bitcast_reduce_fusion.2
  757.9 1.5 fusion.56
  759.4 1.9 fusion.57
  761.3 0.3 copy.115
  761.6 0.2 broadcast_in_dim.143
  761.9 0.8 copy-done.2
  (36 shorter events, 0.3 us)
Async XLA Ops:
  6.5 149.1 %all-gather.6.cloned.1.call-start = ((), (), s32[]{:S(2)}) async-start(), calls=%async_computation.2 | async-start | bytes 2129920 | tf_op jit(solution)/shard_map/all_gather | solution.py:89
  7.3 203.2 %all-gather.4.cloned.1.call-start = ((), (), s32[]{:S(2)}) async-start(), calls=%async_computation.1 | async-start | bytes 9437184 | tf_op jit(solution)/shard_map/all_gather | solution.py:92
  224.0 17.6 %copy-start = (s32[16]{0:T(128)S(1)}, s32[16]{0:T(128)}, u32[]{:S(2)}) copy-start(s32[16]{0:T(128)} %param.11) | copy-start | bytes 196
  224.0 18.1 %copy-start.3 = (s32[2]{0:T(128)S(1)}, s32[2]{0:T(128)}, u32[]{:S(2)}) copy-start(s32[2]{0:T(128)} %param.12) | copy-start | bytes 28
  224.0 500.5 %all-to-all-start = ((bf16[64,2,64,256]{3,2,1,0:T(8,128)(2,1)}), bf16[64,2,64,256]{3,2,1,0:T(8,128)(2,1)}, u32[]{:S(2)}, u32[]{:S(2)}) async-start(bf16[64,2,64,256]{3,2,1,0:T(8,128)(2,1)} %broadcast_select_fusion), calls=%async_computation | async-start | bytes 8388608 | tf_op jit(solution)/shard_map/all_to_all | solution.py:73
  240.0 192.9 %all-gather.8.cloned.1.call-start = ((), (), s32[]{:S(2)}) async-start(), calls=%async_computation.3 | async-start | bytes 2129920 | tf_op jit(solution)/shard_map/all_gather | solution.py:88
  242.1 476.8 %collective-permute-start.1 = (bf16[128,256]{1,0:T(8,128)(2,1)S(1)}, bf16[128,256]{1,0:T(8,128)(2,1)S(1)}, u32[]{:S(2)}, u32[]{:S(2)}) collective-permute-start(bf16[128,256]{1,0:T(8,128)(2,1)S(1)} %get-tuple-element.61), channel_id=1, source_target_pairs={{8,0},{16,8},{24,16},{32,24},{40,32},{48,40},{56,48},{64,56},{72,6... | collective-permute-start | bytes 196616 | tf_op jit(solution)/shard_map/ppermute | solution.py:22
  243.4 475.5 %collective-permute-start = (bf16[128,256]{1,0:T(8,128)(2,1)S(1)}, bf16[128,256]{1,0:T(8,128)(2,1)S(1)}, u32[]{:S(2)}, u32[]{:S(2)}) collective-permute-start(bf16[128,256]{1,0:T(8,128)(2,1)S(1)} %get-tuple-element.62), channel_id=1, source_target_pairs={{0,8},{8,16},{16,24},{24,32},{32,40},{40,48},{48,56},{56,64},{64,7... | collective-permute-start | bytes 196616 | tf_op jit(solution)/shard_map/ppermute | solution.py:21
  742.4 2.4 copy-start.1
  744.9 0.8 copy-start.2
  759.4 2.4 copy-start.1
  761.8 0.8 copy-start.2
Sparse Core Ops, SparseCore 0:
  10.3 145.3 all-gather.5
  157.8 52.5 all-gather.3
  243.8 189.0 all-gather.7
where the time goes:
time: 770 us; the launch traced here: 769 us
  waiting for transfers between devices  386 us (50%)
  blocking collectives  280 us (36%)
  local copies, waits for them, and re-layouts  39.2 us (5%)
  starting transfers between devices  21.9 us (3%)
  matrix products  19 us (2%)
  between operations  13.3 us (2%)
  other arithmetic  9.89 us (1%)
    psum x1, blocking collectives, fetch_blocks(): global_kv = lax.psum(sum_term, 'ctx').astype(jnp.bfloat16)  280 us
    all_gather x1, waiting for transfers between devices, per_device(): lax.all_gather(query_weight, 'ctx', axis=0, tiled=True)  184 us
    all_gather x1, waiting for transfers between devices, per_device(): lax.all_gather(kv_weight, 'ctx', axis=0, tiled=True)  145 us
    all_gather x1, waiting for transfers between devices, per_device(): token_piece = lax.all_gather(tokens, 'tp', axis=0, tiled=True)  54.8 us
    all_to_all x1, starting transfers between devices, fetch_blocks(): lax.all_to_all(outgoing, 'ctx', split_axis=0, concat_axis=0, tiled=True)  16 us
  transfers between devices with their start and end apart: 6, of which 3 were waited for; matrix products, arithmetic and copies ran while one was open for 2% of the time, Pallas kernels for 0%

commit v1 on v0

--- a/solution.py
+++ b/solution.py
@@ -86,7 +86,9 @@
     ctx_index = lax.axis_index("ctx")
     full_query_w, full_kv_w = (
         lax.all_gather(query_weight, "ctx", axis=0, tiled=True),
-        lax.all_gather(kv_weight, "ctx", axis=0, tiled=True),
+        jnp.concatenate(
+            lax.all_to_all(jnp.stack([kv_weight] * lax.axis_size("ctx")), "ctx", 0, 0), axis=0
+        ),
     )
     query_width = full_query_w.shape[1]
     token_piece = lax.all_gather(tokens, "tp", axis=0, tiled=True)

time: 770 us -> 683 us (0.89)
  the two profiles are of different devices: /device:TPU:8 before, /device:TPU:24 now
where the time goes in v1:
time: 683 us; the launch traced here: 682 us
  waiting for transfers between devices  287 us (42%)
  blocking collectives  282 us (41%)
  local copies, waits for them, and re-layouts  40.9 us (6%)
  starting transfers between devices  30.7 us (4%)
  matrix products  18.4 us (3%)
  between operations  15 us (2%)
  other arithmetic  8.55 us (1%)
    psum x1, blocking collectives, fetch_blocks(): global_kv = lax.psum(sum_term, 'ctx').astype(jnp.bfloat16)  282 us
    all_gather x1, waiting for transfers between devices, per_device(): lax.all_gather(query_weight, 'ctx', axis=0, tiled=True)  187 us
    all_to_all x1, waiting for transfers between devices, per_device(): lax.all_to_all(jnp.stack([kv_weight] * lax.axis_size('ctx')), 'ctx', 0, 0)  98.7 us
    all_to_all x1, starting transfers between devices, per_device(): lax.all_to_all(jnp.stack([kv_weight] * lax.axis_size('ctx')), 'ctx', 0, 0)  18.6 us
  transfers between devices with their start and end apart: 6, of which 2 were waited for; matrix products, arithmetic and copies ran while one was open for 2% of the time, Pallas kernels for 0%

profile of v1, /device:TPU:24, one launch (start us, length us, event | category | flops | bytes accessed | tf_op | source)
XLA Modules:
  0.0 682.4 jit_solution(6954795083290051320)
XLA Ops:
  7.4 0.7 all-gather.3.cloned.1.call-update
  8.1 2.4 stack.2
  10.5 18.6 %all-to-all-start = ((bf16[64,64,256]{2,1,0:T(8,128)(2,1)}), bf16[64,64,256]{2,1,0:T(8,128)(2,1)S(1)}, u32[]{:S(2)}, u32[]{:S(2)}) async-start(bf16[64,64,256]{2,1,0:T(8,128)(2,1)} %stack.2), calls=%async_computation | async-start | bytes 4194304 | tf_op jit(solution)/shard_map/all_to_all | solution.py:90
  29.0 0.2 copy.68
  29.3 0.3 reshape.288
  29.5 0.1 copy.72
  29.7 0.2 reduce_window_sum.11
  29.9 0.1 copy.70
  30.0 0.1 copy.69
  30.1 0.1 copy.71
  30.3 0.1 copy.73
  30.3 0.1 reshape.303
  30.5 98.7 %all-to-all-done = bf16[64,64,256]{2,1,0:T(8,128)(2,1)S(1)} async-done(((bf16[64,64,256]{2,1,0:T(8,128)(2,1)}), bf16[64,64,256]{2,1,0:T(8,128)(2,1)S(1)}, u32[]{:S(2)}, u32[]{:S(2)}) %all-to-all-start) | async-done | bytes 2097184 | tf_op jit(solution)/shard_map/all_to_all | solution.py:90
  129.3 5.7 convolution_convert_fusion.1
  135.0 2.7 gather_fusion.1
  137.7 4.5 broadcast_select_fusion
  142.2 6.2 all-to-all-start.1
  148.4 0.0 all-gather.5.cloned.1.call-start
  148.5 0.5 all-gather.5.cloned.1.call-update
  149.0 0.1 pad.1.clone
  149.1 0.1 dynamic-slice_compare_fusion
  149.2 0.1 fusion.35
  149.3 0.1 pad_add_fusion
  149.4 0.1 copy.79
  149.5 0.2 convert_reduce_fusion
  149.7 0.6 gather_fusion
  150.3 0.1 convert_select_fusion
  150.4 1.3 collective-permute-start.1
  151.7 4.5 collective-permute-start
  156.2 187.1 %all-gather.5.cloned.1.call-done = bf16[4096,256]{1,0:T(8,128)(2,1)} async-done(((bf16[64,256]{1,0:T(8,128)(2,1)}), bf16[4096,256]{1,0:T(8,128)(2,1)}) %all-gather.5.cloned.1.call-update) | async-done | bytes 2097168 | tf_op jit(solution)/shard_map/all_gather | solution.py:88
  343.3 6.3 convolution_convert_fusion
  349.6 281.7 %all-reduce.1 = bf16[2,64,256]{2,1,0:T(8,128)(2,1)S(1)} all-reduce(f32[2,64,256]{2,1,0:T(8,128)S(1)} %convert_select_fusion), channel_id=1, replica_groups=mesh['ctx'=64,'tp'=8] {'ctx'}, use_global_device_ids=true, to_apply=%region_0.1 | all-reduce | flops 32768 | bytes 196608 | tf_op jit(solution)/shard_map/psum | solution.py:62
  631.3 0.1 pad_maximum_fusion
  631.4 0.9 constant_dynamic-update-slice_fusion.6
  632.3 0.9 constant_dynamic-update-slice_fusion.5
  633.2 0.9 constant_dynamic-update-slice_fusion.4
  634.0 0.9 constant_dynamic-update-slice_fusion.3
  634.9 0.9 constant_dynamic-update-slice_fusion.2
  635.8 1.1 broadcast_dynamic-update-slice_fusion
  636.9 2.8 gather_fusion.2
  639.7 1.3 constant_dynamic-update-slice_fusion.1
  641.0 34.0 %while.10 = (s32[]{:T(128)}, bf16[2,512,256]{2,1,0:T(8,128)(2,1)}, bf16[2,8,10,64,256]{4,3,2,1,0:T(8,128)(2,1)}, pred[2,8,10]{2,1,0:T(8,128)(4,1)S(1)}, bf16[2,8,64,256]{3,2,1,0:T(8,128)(2,1)S(1)}, /*index=5*/s32[]{:T(128)}) while((s32[]{:T(128)}, bf16[2,512,256]{2,1,0:T(8,128)(2,1)}, bf16[2,8,10,64,256]{4,3,2,1,0:T(8,128)(2,1)}, ...), condition=%wide.region_8.9_spmd, body=%wide.region_5.8_spmd.sunk | while | flops 343537664 | bytes 33575460 | solution.py:130
  641.0 0.1 reshape.325
  641.1 3.6 constant_dynamic-slice_fusion.6
  644.7 3.5 reshape.326
  648.2 3.7 fusion.55
  651.9 1.3 bitcast_reduce_fusion.2
  653.2 1.5 fusion.56
  654.8 0.0 copy-start.2
  654.8 1.9 fusion.57
  656.7 0.3 copy.115
  657.0 0.2 broadcast_in_dim.143
  657.2 0.0 copy-start.3
  657.2 0.8 copy-done.3
  658.0 0.1 reshape.325
  658.1 3.6 constant_dynamic-slice_fusion.6
  661.7 3.5 reshape.326
  665.2 3.7 fusion.55
  668.9 1.3 bitcast_reduce_fusion.2
  670.2 1.5 fusion.56
  671.8 1.9 fusion.57
  673.7 0.3 copy.115
  674.0 0.2 broadcast_in_dim.143
  674.2 0.8 copy-done.3
  (38 shorter events, 0.3 us)
Async XLA Ops:
  7.4 21.7 %copy-start = (s32[1024,3]{0,1:T(4,128)S(1)}, s32[1024,3]{0,1:T(4,128)}, u32[]{:S(2)}) copy-start(s32[1024,3]{0,1:T(4,128)} %param.13) | copy-start | bytes 36868
  7.4 23.1 %copy-start.4 = (s32[2]{0:T(128)S(1)}, s32[2]{0:T(128)}, u32[]{:S(2)}) copy-start(s32[2]{0:T(128)} %param.12) | copy-start | bytes 28
  7.4 121.9 %all-gather.3.cloned.1.call-start = ((), (), s32[]{:S(2)}) async-start(), calls=%async_computation.2 | async-start | bytes 9437184 | tf_op jit(solution)/shard_map/all_gather | solution.py:94
  10.5 118.8 %all-to-all-start = ((bf16[64,64,256]{2,1,0:T(8,128)(2,1)}), bf16[64,64,256]{2,1,0:T(8,128)(2,1)S(1)}, u32[]{:S(2)}, u32[]{:S(2)}) async-start(bf16[64,64,256]{2,1,0:T(8,128)(2,1)} %stack.2), calls=%async_computation | async-start | bytes 4194304 | tf_op jit(solution)/shard_map/all_to_all | solution.py:90
  142.2 7.0 %copy-start.1 = (s32[16]{0:T(128)S(1)}, s32[16]{0:T(128)}, u32[]{:S(2)}) copy-start(s32[16]{0:T(128)} %param.11) | copy-start | bytes 196
  142.2 494.7 %all-to-all-start.1 = ((bf16[64,2,64,256]{3,2,1,0:T(8,128)(2,1)}), bf16[64,2,64,256]{3,2,1,0:T(8,128)(2,1)}, u32[]{:S(2)}, u32[]{:S(2)}) async-start(bf16[64,2,64,256]{3,2,1,0:T(8,128)(2,1)} %broadcast_select_fusion), calls=%async_computation.1 | async-start | bytes 8388608 | tf_op jit(solution)/shard_map/all_to_all | solution.py:73
  148.4 194.8 %all-gather.5.cloned.1.call-start = ((), (), s32[]{:S(2)}) async-start(), calls=%async_computation.3 | async-start | bytes 2129920 | tf_op jit(solution)/shard_map/all_gather | solution.py:88
  150.4 480.9 %collective-permute-start.1 = (bf16[128,256]{1,0:T(8,128)(2,1)S(1)}, bf16[128,256]{1,0:T(8,128)(2,1)S(1)}, u32[]{:S(2)}, u32[]{:S(2)}) collective-permute-start(bf16[128,256]{1,0:T(8,128)(2,1)S(1)} %get-tuple-element.61), channel_id=1, source_target_pairs={{8,0},{16,8},{24,16},{32,24},{40,32},{48,40},{56,48},{64,56},{72,6... | collective-permute-start | bytes 196616 | tf_op jit(solution)/shard_map/ppermute | solution.py:22
  151.7 479.6 %collective-permute-start = (bf16[128,256]{1,0:T(8,128)(2,1)S(1)}, bf16[128,256]{1,0:T(8,128)(2,1)S(1)}, u32[]{:S(2)}, u32[]{:S(2)}) collective-permute-start(bf16[128,256]{1,0:T(8,128)(2,1)S(1)} %get-tuple-element.62), channel_id=1, source_target_pairs={{0,8},{8,16},{16,24},{24,32},{32,40},{40,48},{48,56},{56,64},{64,7... | collective-permute-start | bytes 196616 | tf_op jit(solution)/shard_map/ppermute | solution.py:21
  654.8 2.4 copy-start.2
  657.2 0.8 copy-start.3
  671.8 2.4 copy-start.2
  674.2 0.8 copy-start.3
Sparse Core Ops, SparseCore 0:
  10.3 59.7 all-gather.2
Sparse Core Ops, SparseCore 1:
  151.9 191.4 all-gather.4
